TPU v7x, 512 devices: a whole 4x8x8 slice. The times are simulated.
512 devices in a mesh: seqa: 16 (over x, z_lo), seqb: 32 (over y, z_hi, core).
Axes of the slice: x: 4, y: 8, z: 8 (z_hi: 2, z_lo: 4; z = z_hi * 4 + z_lo), core: 2. Of those that a mesh axis runs over, the one named last changes fastest.
Arguments:
- query_rows: bfloat16 [131072, 1024], P(('seqa', 'seqb')), may hold values from -256 to 256
- key_rows: bfloat16 [131072, 1024], P(('seqa', 'seqb')), may hold values from -16 to 16
- value_rows: bfloat16 [131072, 1024], P(('seqa', 'seqb')), may hold values from -16 to 16
Outputs:
- attended: bfloat16 [131072, 1024], P(('seqa', 'seqb'))
All inputs are finite; a program needn't handle non-finite values.
Results may differ from a plain program's by a relative error of at most 0.0027.
Values may be sent and summed in bfloat16 or wider, within the bound.
A program may use at most 64 MiB of HBM per device.

v0:
```python
import jax
import jax.numpy as jnp
from jax import lax
from jax.sharding import PartitionSpec as P

HEADS = 8
HEAD_DIM = 128
HALF_WIN = 256


def partner_2(x, axis, bit):
    return lax.ppermute(x, axis, [(i, i ^ 1 << bit) for i in range(lax.axis_size(axis))])


def extended(cells, sides, width):
    for axis, dim in sides:
        count = lax.axis_size(axis)
        ends = count - 1
        head = lax.slice_in_dim(cells, 0, width, axis=dim)
        tail = lax.slice_in_dim(cells, cells.shape[dim] - width, cells.shape[dim], axis=dim)
        cells = jnp.concatenate(
            [
                lax.ppermute(tail, axis, [(i, (i + 1) % count) for i in range(ends)]),
                cells,
                lax.ppermute(head, axis, [((i + 1) % count, i) for i in range(ends)]),
            ],
            axis=dim,
        )
    return cells


def pooled_means(stacked):
    count = stacked.shape[1] // 4
    summed = stacked.astype(jnp.float32).reshape(2, count, 4, stacked.shape[2]).mean(axis=2)
    return summed.astype(jnp.bfloat16)


def ordered_join(mine, partner, upper):
    return jnp.where(
        upper, jnp.concatenate([partner, mine], axis=1), jnp.concatenate([mine, partner], axis=1)
    )


def grow_local(stacked):
    position = lax.axis_index("seqb")
    for bit_index in range(3):
        partner = partner_2(stacked, "seqb", bit_index)
        stacked = ordered_join(stacked, partner, position >> bit_index & 1 == 1)
    return stacked


def grow_outer(stacked):
    position = lax.axis_index("seqa")
    for bit_index in range(2):
        partner = partner_2(stacked, "seqa", bit_index)
        stacked = ordered_join(stacked, partner, position >> bit_index & 1 == 1)
    return stacked


def row_scores(queries, keys):
    return lax.dot_general(
        queries, keys, (((1,), (1,)), ((), ())), preferred_element_type=jnp.float32
    )


def local(query_rows, key_rows, value_rows):
    tok_rows = query_rows.shape[0]
    stacked = jnp.stack([key_rows, value_rows])
    near_rows = extended(stacked, ((("seqa", "seqb"), 1),), HALF_WIN)
    own_one = pooled_means(stacked)
    level_one = grow_local(own_one)
    level_two = lax.all_gather(pooled_means(own_one), "seqb", axis=1, tiled=True)
    group_three = pooled_means(level_two)
    level_three = grow_outer(group_three)
    level_four = lax.all_gather(pooled_means(group_three), "seqa", axis=1, tiled=True)
    far_rows = jnp.concatenate([level_one, level_two, level_three, level_four], axis=1)
    near_count = tok_rows + 2 * HALF_WIN
    first_row = lax.axis_index(("seqa", "seqb")) * tok_rows
    all_tokens = tok_rows * lax.axis_size("seqa") * lax.axis_size("seqb")
    column = jnp.arange(near_count, dtype=jnp.int32)[None, :]
    row_index = jnp.arange(tok_rows, dtype=jnp.int32)[:, None]
    key_position = first_row - HALF_WIN + column
    near_allowed = (column >= row_index) & (column <= row_index + 2 * HALF_WIN - 1)
    near_allowed = near_allowed & (key_position >= 0) & (key_position < all_tokens)
    near_bias = jnp.where(near_allowed, 0.0, -1e30).astype(jnp.float32)
    score_scale = 1.0 / HEAD_DIM**0.5
    results = []
    for head in range(HEADS):
        lower = head * HEAD_DIM
        upper = lower + HEAD_DIM
        queries = query_rows[:, lower:upper]
        near_scores = row_scores(queries, near_rows[0, :, lower:upper]) * score_scale + near_bias
        far_scores = row_scores(queries, far_rows[0, :, lower:upper]) * score_scale
        highest = jnp.maximum(
            jnp.max(near_scores, axis=1, keepdims=True), jnp.max(far_scores, axis=1, keepdims=True)
        )
        near_expo = jnp.exp(near_scores - highest)
        far_expo = jnp.exp(far_scores - highest)
        denominator = jnp.sum(near_expo, axis=1, keepdims=True) + jnp.sum(
            far_expo, axis=1, keepdims=True
        )
        mixed = jnp.dot(
            near_expo.astype(jnp.bfloat16),
            near_rows[1, :, lower:upper],
            preferred_element_type=jnp.float32,
        )
        mixed = mixed + jnp.dot(
            far_expo.astype(jnp.bfloat16),
            far_rows[1, :, lower:upper],
            preferred_element_type=jnp.float32,
        )
        results.append(mixed / denominator)
    return jnp.concatenate(results, axis=1).astype(jnp.bfloat16)


def solution(mesh):
    return jax.shard_map(
        local,
        mesh=mesh,
        in_specs=(P(("seqa", "seqb"), None), P(("seqa", "seqb"), None), P(("seqa", "seqb"), None)),
        out_specs=P(("seqa", "seqb"), None),
        check_vma=False,
    )
```

profile of v0, /device:TPU:49, one launch (start us, length us, event | category | flops | bytes accessed | tf_op | source)
XLA Modules:
  0.0 346.5 jit_solution(13911394192303098383)
XLA Ops:
  6.5 1.2 stack.19
  7.8 1.2 stack.18
  9.0 1.4 convert_reduce_fusion
  11.0 0.6 multiply_convert_fusion.3
  11.7 2.6 collective-permute-start.2
  14.3 95.2 %all-gather.3.cloned.1.call-done = bf16[2,512,1024]{2,1,0:T(8,128)(2,1)} async-done(((bf16[2,16,1024]{2,1,0:T(8,128)(2,1)}), bf16[2,512,1024]{2,1,0:T(8,128)(2,1)}) %all-gather.3.cloned.1.call-update) | async-done | bytes 2097168 | tf_op jit(solution)/shard_map/all_gather | solution.py:72
  109.5 4.9 %reshape.141 = f32[2,128,4,1024]{3,2,1,0:T(4,128)} reshape(bf16[2,512,1024]{2,1,0:T(8,128)(2,1)} %all-gather.3.cloned.1.call-done) | data formatting | bytes 6291456 | tf_op jit(solution)/shard_map/reshape | solution.py:34
  114.4 4.8 %reduce_sum.182 = f32[2,128,1024]{2,1,0:T(8,128)S(1)} reduce(f32[2,128,4,1024]{3,2,1,0:T(4,128)} %reshape.141, f32[]{:T(128)} %constant.15.clone.1), dimensions={2}, to_apply=%region_3.4 | reduce | flops 786432 | bytes 5242884 | tf_op jit(solution)/shard_map/reduce_sum | solution.py:34
  120.3 0.7 multiply_convert_fusion.2
  121.0 1.1 pad_maximum_fusion.2
  122.1 2.2 collective-permute-start.1
  124.3 7.3 %collective-permute-start = (bf16[2,256,1024]{2,1,0:T(8,128)(2,1)}, bf16[2,256,1024]{2,1,0:T(8,128)(2,1)}, u32[]{:S(2)}, u32[]{:S(2)}) collective-permute-start(bf16[2,256,1024]{2,1,0:T(8,128)(2,1)} %pad_maximum_fusion.2), channel_id=1, source_target_pairs={{0,1},{1,2},{2,3},{3,4},{4,5},{5,6},{6,7},{7,8},{8,9},{9,10},{10,1... | collective-permute-start | bytes 3145736 | tf_op jit(solution)/shard_map/ppermute | solution.py:23
  131.7 1.9 collective-permute-start.3
  133.7 75.4 %collective-permute-done.3 = bf16[2,128,1024]{2,1,0:T(8,128)(2,1)S(1)} collective-permute-done((bf16[2,128,1024]{2,1,0:T(8,128)(2,1)S(1)}, bf16[2,128,1024]{2,1,0:T(8,128)(2,1)S(1)}, u32[]{:S(2)}, u32[]{:S(2)}) %collective-permute-start.3) | collective-permute-done | bytes 524320 | tf_op jit(solution)/shard_map/ppermute | solution.py:12
  209.6 24.0 %collective-permute-start.4 = (bf16[2,256,1024]{2,1,0:T(8,128)(2,1)S(1)}, bf16[2,256,1024]{2,1,0:T(8,128)(2,1)S(1)}, u32[]{:S(2)}, u32[]{:S(2)}) collective-permute-start(bf16[2,256,1024]{2,1,0:T(8,128)(2,1)S(1)} %maximum_select_fusion.2), channel_id=1, source_target_pairs={{0,4},{1,5},{2,6},{3,7},{4,0},{5,1},{6,2},{7,3},{8,12},{9,13},{10,... | collective-permute-start | bytes 3145736 | tf_op jit(solution)/shard_map/ppermute | solution.py:12
  233.7 1.8 pad_maximum_fusion.1
  235.5 1.6 fusion.125
  237.1 1.9 collective-permute-start.5
  239.0 1.3 fusion.127
  240.3 1.3 fusion.129
  241.7 1.3 fusion.131
  242.9 10.7 %collective-permute-done.5 = bf16[2,128,1024]{2,1,0:T(8,128)(2,1)S(1)} collective-permute-done((bf16[2,128,1024]{2,1,0:T(8,128)(2,1)S(1)}, bf16[2,128,1024]{2,1,0:T(8,128)(2,1)S(1)}, u32[]{:S(2)}, u32[]{:S(2)}) %collective-permute-start.5) | collective-permute-done | bytes 524320 | tf_op jit(solution)/shard_map/ppermute | solution.py:12
  254.1 16.0 %collective-permute-start.6 = (bf16[2,256,1024]{2,1,0:T(8,128)(2,1)S(1)}, bf16[2,256,1024]{2,1,0:T(8,128)(2,1)S(1)}, u32[]{:S(2)}, u32[]{:S(2)}) collective-permute-start(bf16[2,256,1024]{2,1,0:T(8,128)(2,1)S(1)} %maximum_select_fusion.3), channel_id=1, source_target_pairs={{0,64},{32,96},{64,0},{96,32},{128,192},{160,224},{192,128},{224,1... | collective-permute-start | bytes 3145736 | tf_op jit(solution)/shard_map/ppermute | solution.py:12
  270.1 1.3 fusion.133
  271.4 1.2 fusion.135
  272.6 1.3 fusion.137
  274.3 2.3 maximum_select_fusion
  276.6 38.6 %collective-permute-done.6 = bf16[2,256,1024]{2,1,0:T(8,128)(2,1)S(1)} collective-permute-done((bf16[2,256,1024]{2,1,0:T(8,128)(2,1)S(1)}, bf16[2,256,1024]{2,1,0:T(8,128)(2,1)S(1)}, u32[]{:S(2)}, u32[]{:S(2)}) %collective-permute-start.6) | collective-permute-done | bytes 1048608 | tf_op jit(solution)/shard_map/ppermute | solution.py:12
  315.2 2.4 maximum_select_fusion.1
  317.6 3.9 %pad_maximum_fusion = bf16[2,2048,1024]{2,1,0:T(8,128)(2,1)S(1)} fusion(bf16[2,512,1024]{2,1,0:T(8,128)(2,1)} %all-gather.5.cloned.1.call-done, bf16[2,512,1024]{2,1,0:T(8,128)(2,1)} %maximum_select_fusion.1, bf16[2,512,1024]{2,1,0:T(8,128)(2,1)S(1)} %copy-done, bf16[2,512,1024]{2,1,0:T(8,128)(2,1)} %maximum_select_fusion), kind=kLoop, calls=%fused_computation | loop fusion | flops 33554432 | bytes 16777216 | tf_op jit(solution)/shard_map/concatenate | solution.py:76
  335.2 0.8 copy-done.4
  338.7 1.0 copy.8
  (102 shorter events, 19.2 us)
Async XLA Ops:
  6.5 103.0 %all-gather.3.cloned.1.call-start = ((), (), s32[]{:S(2)}) async-start(), calls=%async_computation | async-start | bytes 2162688 | tf_op jit(solution)/shard_map/all_gather | solution.py:72
  11.7 305.9 %all-gather.5.cloned.1.call-start = ((), (), s32[]{:S(2)}) async-start(), calls=%async_computation.1 | async-start | bytes 2228224 | tf_op jit(solution)/shard_map/all_gather | solution.py:75
  11.7 119.9 %collective-permute-start.2 = (bf16[2,64,1024]{2,1,0:T(8,128)(2,1)S(1)}, bf16[2,64,1024]{2,1,0:T(8,128)(2,1)S(1)}, u32[]{:S(2)}, u32[]{:S(2)}) collective-permute-start(bf16[2,64,1024]{2,1,0:T(8,128)(2,1)S(1)} %multiply_convert_fusion.1), channel_id=1, source_target_pairs={{0,1},{1,0},{2,3},{3,2},{4,5},{5,4},{6,7},{7,6},{8,9},{9,8},{10,11... | collective-permute-start | bytes 786440 | tf_op jit(solution)/shard_map/ppermute | solution.py:12
  119.3 1.7 copy-start.1
  119.3 1.7 copy-start.2
  122.1 111.6 %collective-permute-start.1 = (bf16[2,256,1024]{2,1,0:T(8,128)(2,1)}, bf16[2,256,1024]{2,1,0:T(8,128)(2,1)}, u32[]{:S(2)}, u32[]{:S(2)}) collective-permute-start(bf16[2,256,1024]{2,1,0:T(8,128)(2,1)} %pad_maximum_fusion.2), channel_id=1, source_target_pairs={{1,0},{2,1},{3,2},{4,3},{5,4},{6,5},{7,6},{8,7},{9,8},{10,9},{11,1... | collective-permute-start | bytes 3145736 | tf_op jit(solution)/shard_map/ppermute | solution.py:25
  124.3 109.4 %collective-permute-start = (bf16[2,256,1024]{2,1,0:T(8,128)(2,1)}, bf16[2,256,1024]{2,1,0:T(8,128)(2,1)}, u32[]{:S(2)}, u32[]{:S(2)}) collective-permute-start(bf16[2,256,1024]{2,1,0:T(8,128)(2,1)} %pad_maximum_fusion.2), channel_id=1, source_target_pairs={{0,1},{1,2},{2,3},{3,4},{4,5},{5,6},{6,7},{7,8},{8,9},{9,10},{10,1... | collective-permute-start | bytes 3145736 | tf_op jit(solution)/shard_map/ppermute | solution.py:23
  131.7 77.4 %collective-permute-start.3 = (bf16[2,128,1024]{2,1,0:T(8,128)(2,1)S(1)}, bf16[2,128,1024]{2,1,0:T(8,128)(2,1)S(1)}, u32[]{:S(2)}, u32[]{:S(2)}) collective-permute-start(bf16[2,128,1024]{2,1,0:T(8,128)(2,1)S(1)} %maximum_select_fusion.4), channel_id=1, source_target_pairs={{0,2},{1,3},{2,0},{3,1},{4,6},{5,7},{6,4},{7,5},{8,10},{9,11},{10,... | collective-permute-start | bytes 1572872 | tf_op jit(solution)/shard_map/ppermute | solution.py:12
  209.6 25.9 %copy-start.12 = (bf16[256,1024]{1,0:T(8,128)(2,1)S(1)}, bf16[256,1024]{1,0:T(8,128)(2,1)}, u32[]{:S(2)}) copy-start(bf16[256,1024]{1,0:T(8,128)(2,1)} %param.3) | copy-start | bytes 1572868
  209.6 64.7 %collective-permute-start.4 = (bf16[2,256,1024]{2,1,0:T(8,128)(2,1)S(1)}, bf16[2,256,1024]{2,1,0:T(8,128)(2,1)S(1)}, u32[]{:S(2)}, u32[]{:S(2)}) collective-permute-start(bf16[2,256,1024]{2,1,0:T(8,128)(2,1)S(1)} %maximum_select_fusion.2), channel_id=1, source_target_pairs={{0,4},{1,5},{2,6},{3,7},{4,0},{5,1},{6,2},{7,3},{8,12},{9,13},{10,... | collective-permute-start | bytes 3145736 | tf_op jit(solution)/shard_map/ppermute | solution.py:12
  235.5 38.4 %copy-start.3 = (bf16[2,768,1024]{2,1,0:T(8,128)(2,1)}, bf16[2,768,1024]{2,1,0:T(8,128)(2,1)S(1)}, u32[]{:S(2)}) copy-start(bf16[2,768,1024]{2,1,0:T(8,128)(2,1)S(1)} %pad_maximum_fusion.1) | copy-start | bytes 9437188
  237.1 16.6 %collective-permute-start.5 = (bf16[2,128,1024]{2,1,0:T(8,128)(2,1)S(1)}, bf16[2,128,1024]{2,1,0:T(8,128)(2,1)S(1)}, u32[]{:S(2)}, u32[]{:S(2)}) collective-permute-start(bf16[2,128,1024]{2,1,0:T(8,128)(2,1)S(1)} %multiply_convert_fusion), channel_id=1, source_target_pairs={{0,32},{32,0},{64,96},{96,64},{128,160},{160,128},{192,224},{224,1... | collective-permute-start | bytes 1572872 | tf_op jit(solution)/shard_map/ppermute | solution.py:12
  254.1 61.1 %collective-permute-start.6 = (bf16[2,256,1024]{2,1,0:T(8,128)(2,1)S(1)}, bf16[2,256,1024]{2,1,0:T(8,128)(2,1)S(1)}, u32[]{:S(2)}, u32[]{:S(2)}) collective-permute-start(bf16[2,256,1024]{2,1,0:T(8,128)(2,1)S(1)} %maximum_select_fusion.3), channel_id=1, source_target_pairs={{0,64},{32,96},{64,0},{96,32},{128,192},{160,224},{192,128},{224,1... | collective-permute-start | bytes 3145736 | tf_op jit(solution)/shard_map/ppermute | solution.py:12
  276.6 41.0 %copy-start = (bf16[2,512,1024]{2,1,0:T(8,128)(2,1)S(1)}, bf16[2,512,1024]{2,1,0:T(8,128)(2,1)}, u32[]{:S(2)}) copy-start(bf16[2,512,1024]{2,1,0:T(8,128)(2,1)} %all-gather.3.cloned.1.call-done) | copy-start | bytes 6291460
  331.9 1.1 copy-start.11
  332.4 1.2 copy-start.9
  332.4 1.4 copy-start.7
  332.4 1.6 copy-start.5
  332.8 1.6 copy-start.10
  332.8 1.8 copy-start.8
  333.2 1.7 copy-start.6
  334.0 2.1 copy-start.4
Sparse Core Ops, SparseCore 0:
  11.8 97.7 all-gather.2
  121.1 124.3 all-gather.4
where the time goes:
time: 347 us
  waiting for transfers between devices  220 us (63%)
  starting transfers between devices  55.9 us (16%)
  other arithmetic  25.4 us (7%)
  matrix products  20.3 us (6%)
  between operations  14 us (4%)
  local copies, waits for them, and re-layouts  10.8 us (3%)
    ppermute x5, waiting for transfers between devices, partner_2(): lax.ppermute(x, axis, [(i, i ^ 1 << bit) for i in range(lax.axis_size(axi...  125 us
    all_gather x1, waiting for transfers between devices, local(): lax.all_gather(pooled_means(own_one), 'seqb', axis=1, tiled=True)  95.2 us
    ppermute x5, starting transfers between devices, partner_2(): lax.ppermute(x, axis, [(i, i ^ 1 << bit) for i in range(lax.axis_size(axi...  46.4 us
    dot_general x16, matrix products, row_scores(): lax.dot_general(queries, keys, (((1,), (1,)), ((), ())), preferred_elemen...  13.9 us
    ppermute x1, starting transfers between devices, extended(): lax.ppermute(tail, axis, [(i, (i + 1) % count) for i in range(ends)])  7.28 us
    reduce_sum x4, other arithmetic, pooled_means(): stacked.astype(jnp.float32).reshape(2, count, 4, stacked.shape[2])  7.17 us
  transfers between devices with their start and end apart: 9, of which 4 were waited for; matrix products, arithmetic and copies ran while one was open for 9% of the time, Pallas kernels for 0%

commit v1 on v0

v1 whole, which is shorter than its diff:
```python
import functools

import jax
import jax.numpy as jnp
from jax import lax
from jax.experimental import pallas as pl
from jax.experimental.pallas import tpu as pltpu
from jax.sharding import PartitionSpec as P

MESH = pl.DeviceIdType.MESH
BF16, F32 = jnp.bfloat16, jnp.float32

HEAD_DIM = 128
BLOCK = 256
NX, NY, NZ, NZ_LO, N_HI = 4, 8, 8, 4, 2
CHIPS = 256
LOCAL_HEADS = 4
COLS = LOCAL_HEADS * HEAD_DIM
EXP2_SCALE = 1.4426950408889634 / HEAD_DIM**0.5
MASKED = -1e30


def pool_matrix(rows, columns):
    row = lax.broadcasted_iota(jnp.int32, (rows, columns), 0)
    column = lax.broadcasted_iota(jnp.int32, (rows, columns), 1)
    return jnp.where((column >> 2) == row, 0.25, 0.0).astype(BF16)


def matmul(a, b):
    return jnp.dot(a, b, preferred_element_type=F32)


def kernel(
    q_hbm, k_hbm, v_hbm, o_hbm,
    near, queries, l1, l2, l3, l4, tile, acc, top, den, result,
    loc_sem, sib_s, sib_r, near_s, near_r, l2z_s, l2z_r, l3z_s, l3z_r, l1_s, l1_r,
    ring2_s, ring2_r, ring3_s, ring3_r, l4_s, l4_r, out_loc, out_s, out_r,
):
    seqa, seqb = lax.axis_index("seqa"), lax.axis_index("seqb")
    x, z_lo = seqa // NZ_LO, seqa % NZ_LO
    y, hi, core = seqb // 4, (seqb // 2) % 2, seqb % 2
    z = hi * NZ_LO + z_lo
    chip = seqa * 16 + seqb // 2

    def at_z(d):
        other = (z + d) % NZ
        return (x * NZ_LO + other % NZ_LO, (y * 2 + other // NZ_LO) * 2 + core)

    def at_y(d):
        return (seqa, (((y + d) % NY) * 2 + hi) * 2 + core)

    def at_x(d):
        return (((x + d) % NX) * NZ_LO + z_lo, seqb)

    def at_chip(c, which):
        return (c // 16, (c % 16) * 2 + which)

    sibling = (seqa, seqb + 1 - 2 * core)
    before, after = (chip + CHIPS - 1) % CHIPS, (chip + 1) % CHIPS
    y_pair = (seqa, ((y + 1 - 2 * (y % 2)) * 2 + hi) * 2 + core)
    y_par = y % 2

    barrier = pltpu.get_barrier_semaphore()
    partners = [sibling, at_chip(before, core), at_chip(after, core)]
    partners += [at_z(d) for d in (1, 2, 3, 5, 6, 7)]
    partners += [at_y(d) for d in (1, 7)] + [at_x(d) for d in (1, 2, 3)]
    for partner in partners:
        pl.semaphore_signal(barrier, inc=1, device_id=partner, device_id_type=MESH)
    pl.semaphore_wait(barrier, len(partners))

    def remote(src, dst, s, r, device):
        return pltpu.make_async_remote_copy(
            src_ref=src, dst_ref=dst, send_sem=s, recv_sem=r, device_id=device, device_id_type=MESH
        )

    mine = pl.ds(pl.multiple_of(core * COLS, COLS), COLS)
    theirs = pl.ds(pl.multiple_of((1 - core) * COLS, COLS), COLS)
    own_rows = pl.ds(pl.multiple_of(core * BLOCK, BLOCK), BLOCK)
    sib_rows = pl.ds(pl.multiple_of((1 - core) * BLOCK, BLOCK), BLOCK)
    own_near = pl.ds(pl.multiple_of(BLOCK + core * BLOCK, BLOCK), BLOCK)
    sib_near = pl.ds(pl.multiple_of(2 * BLOCK - core * BLOCK, BLOCK), BLOCK)

    sib = [
        remote(k_hbm.at[:, theirs], near.at[0, own_near], sib_s.at[0], sib_r.at[0], sibling),
        remote(v_hbm.at[:, theirs], near.at[1, own_near], sib_s.at[1], sib_r.at[1], sibling),
        remote(q_hbm.at[:, theirs], queries.at[own_rows], sib_s.at[2], sib_r.at[2], sibling),
    ]
    loc = [
        pltpu.make_async_copy(k_hbm.at[:, mine], near.at[0, own_near], loc_sem.at[0]),
        pltpu.make_async_copy(v_hbm.at[:, mine], near.at[1, own_near], loc_sem.at[1]),
        pltpu.make_async_copy(q_hbm.at[:, mine], queries.at[own_rows], loc_sem.at[2]),
    ]
    for copy in (sib[0], sib[1], loc[0], loc[1], sib[2], loc[2]):
        copy.start()

    own_to = at_chip(lax.rem(chip + CHIPS - 1 + 2 * core, CHIPS), core)
    sib_to = at_chip(lax.rem(chip + CHIPS + 1 - 2 * core, CHIPS), core)

    def near_copy(second, head, t):
        columns = pl.ds(head * HEAD_DIM, HEAD_DIM)
        if second:
            src = near.at[t, sib_near, columns]
            side, device = core, sib_to
        else:
            src = near.at[t, own_near, columns]
            side, device = 1 - core, own_to
        rows = pl.ds(pl.multiple_of(side * 3 * BLOCK, BLOCK), BLOCK)
        return remote(
            src, near.at[t, rows, columns],
            near_s.at[second, head, t], near_r.at[side, head, t], device,
        )

    loc[0].wait()
    near_first = near_copy(0, 0, 0)
    near_first.start()
    loc[1].wait()
    sib[0].wait_recv()
    sib[1].wait_recv()

    tiles = []
    for t in range(2):
        one = matmul(pool_matrix(128, 512), near[t, BLOCK : 3 * BLOCK, :]).astype(BF16)
        l1[t, y_par, hi] = one
        two = matmul(pool_matrix(32, 128), one).astype(BF16)
        l2[t, y, hi] = two
        tiles.append(matmul(pool_matrix(16, 32), two)[:8])
    tile[z] = jnp.concatenate(tiles, axis=0).astype(BF16)

    l3z = [
        remote(tile.at[z], tile.at[z], l3z_s.at[d], l3z_r.at[d], at_z(d)) for d in range(1, NZ)
    ]
    for copy in l3z:
        copy.start()
    l2z = remote(l2.at[:, y, hi], l2.at[:, y, hi], l2z_s.at[0], l2z_r.at[0], at_z(4))
    l2z.start()
    own_one = l1.at[:, y_par, hi]
    l1y = remote(own_one, own_one, l1_s.at[1], l1_r.at[1], y_pair)
    l1y.start()
    l1z = remote(own_one, own_one, l1_s.at[0], l1_r.at[0], at_z(4))
    l1z.start()
    near_rest = [
        near_copy(second, head, t)
        for head in range(LOCAL_HEADS)
        for second in range(2)
        for t in range(2)
        if (second, head, t) != (0, 0, 0)
    ]

    def attend(head, half, keys, values, allowed, first):
        columns = pl.ds(pl.multiple_of(head * HEAD_DIM, HEAD_DIM), HEAD_DIM)
        q = queries[pl.ds(pl.multiple_of(half * BLOCK, BLOCK), BLOCK), columns]
        scores = lax.dot_general(
            q, keys, (((1,), (1,)), ((), ())), preferred_element_type=F32
        )
        if allowed is not None:
            scores = jnp.where(allowed, scores, MASKED)
        highest = jnp.max(scores, axis=1, keepdims=True)
        slot = head * 2 + half
        if not first:
            old = top[slot]
            highest = jnp.maximum(highest, old)
        weights = jnp.exp2((scores - highest) * EXP2_SCALE)
        total = jnp.sum(weights, axis=1, keepdims=True)
        mixed = matmul(weights.astype(BF16), values)
        if not first:
            shrink = jnp.exp2((old - highest) * EXP2_SCALE)
            total = total + den[slot] * shrink
            mixed = mixed + acc[slot] * shrink
        top[slot] = highest
        den[slot] = total
        acc[slot] = mixed

    def head_columns(head):
        return pl.ds(pl.multiple_of(head * HEAD_DIM, HEAD_DIM), HEAD_DIM)

    loc[2].wait()
    sib[2].wait_recv()

    def inner(i, carry):
        head, half = i // 2, i % 2
        columns = head_columns(head)
        row = lax.broadcasted_iota(jnp.int32, (BLOCK, 2 * BLOCK), 0) + half * BLOCK
        key = lax.broadcasted_iota(jnp.int32, (BLOCK, 2 * BLOCK), 1)
        allowed = (key >= row - BLOCK) & (key <= row + BLOCK - 1)
        attend(
            head, half, near[0, BLOCK : 3 * BLOCK, columns], near[1, BLOCK : 3 * BLOCK, columns],
            allowed, True,
        )
        return carry

    lax.fori_loop(0, 2 * LOCAL_HEADS, inner, 0)

    for copy in l3z:
        copy.wait_recv()
    for t in range(2):
        rows = [tile[i].astype(F32)[8 * t : 8 * t + 8] for i in range(NZ)]
        l3[t, y] = jnp.concatenate(rows, axis=0).astype(BF16)

    l4_copies = []

    def send_four(j, chunk):
        for t in range(2):
            l4[t, x, chunk] = matmul(pool_matrix(16, 64), l3[t, chunk]).astype(BF16)
        part = l4.at[:, x, chunk]
        for d in range(1, NX):
            copy = remote(part, part, l4_s.at[j, d], l4_r.at[j, d], at_x(d))
            copy.start()
            l4_copies.append(copy)

    def ring_step(buf, send, recv, s):
        up, down = (y - (s - 1) + NY) % NY, (y + s - 1) % NY
        if s < 4:
            up, down = buf.at[:, up], buf.at[:, down]
        else:
            up, down = buf.at[0, up], buf.at[1, down]
        copies = [
            remote(up, up, send.at[s - 1, 0], recv.at[s - 1, 0], at_y(1)),
            remote(down, down, send.at[s - 1, 1], recv.at[s - 1, 1], at_y(NY - 1)),
        ]
        for copy in copies:
            copy.start()
        return copies

    ring3 = ring_step(l3, ring3_s, ring3_r, 1)
    send_four(0, y)
    l2z.wait_recv()
    ring2 = ring_step(l2, ring2_s, ring2_r, 1)
    for copy in near_rest:
        copy.start()
    finished = list(ring3) + list(ring2)
    for s in range(1, 5):
        for copy in ring3:
            copy.wait_recv()
        if s < 4:
            ring3 = ring_step(l3, ring3_s, ring3_r, s + 1)
            finished += ring3
            send_four(2 * s - 1, (y - s + NY) % NY)
            send_four(2 * s, (y + s) % NY)
        else:
            send_four(7, (y + 4) % NY)
        for copy in ring2:
            copy.wait_recv()
        if s < 4:
            ring2 = ring_step(l2, ring2_s, ring2_r, s + 1)
            finished += ring2
        if s == 2:
            l1z.wait_recv()
            other_one = l1.at[:, y_par, 1 - hi]
            l1zy = remote(other_one, other_one, l1_s.at[2], l1_r.at[2], y_pair)
            l1zy.start()

    def far(buf):
        def body(i, carry):
            head, half = i // 2, i % 2
            index = (slice(None),) * (len(buf.shape) - 2) + (head_columns(head),)
            keys = buf[(0,) + index].reshape(512, HEAD_DIM)
            values = buf[(1,) + index].reshape(512, HEAD_DIM)
            attend(head, half, keys, values, None, False)
            return carry

        lax.fori_loop(0, 2 * LOCAL_HEADS, body, 0)

    far(l3)
    far(l2)
    l1y.wait_recv()
    l1zy.wait_recv()
    far(l1)
    for copy in l4_copies:
        copy.wait_recv()
    far(l4)

    out = []
    for head in range(LOCAL_HEADS):
        for t in range(2):
            for second in range(2):
                near_copy(second, head, t).wait_recv()
        columns = pl.ds(head * HEAD_DIM, HEAD_DIM)
        for half in range(2):
            edge = pl.ds(half * 3 * BLOCK, BLOCK)
            row = lax.broadcasted_iota(jnp.int32, (BLOCK, BLOCK), 0)
            key = lax.broadcasted_iota(jnp.int32, (BLOCK, BLOCK), 1)
            if half == 0:
                allowed = (key >= row) & (chip > 0)
            else:
                allowed = (key < row) & (chip < CHIPS - 1)
            attend(head, half, near[0, edge, columns], near[1, edge, columns], allowed, False)
            slot = head * 2 + half
            result[half, :, columns] = (acc[slot] / den[slot]).astype(BF16)
        place = pl.ds(pl.multiple_of(core * COLS + head * HEAD_DIM, HEAD_DIM), HEAD_DIM)
        away = remote(
            result.at[1 - core, :, columns], o_hbm.at[:, place],
            out_s.at[head], out_r.at[head], sibling,
        )
        away.start()
        here = pltpu.make_async_copy(
            result.at[core, :, columns], o_hbm.at[:, place], out_loc.at[head]
        )
        here.start()
        out += [(away, here)]
    for copy in sib + l3z + [l2z, l1y, l1z, l1zy] + [near_first] + near_rest + finished + l4_copies:
        copy.wait_send()
    for away, here in out:
        here.wait()
        away.wait()


def local(query_rows, key_rows, value_rows):
    any_space = pl.BlockSpec(memory_space=pl.ANY)
    dma = pltpu.SemaphoreType.DMA
    return pl.pallas_call(
        kernel,
        out_shape=jax.ShapeDtypeStruct(query_rows.shape, query_rows.dtype),
        in_specs=[any_space] * 3,
        out_specs=any_space,
        scratch_shapes=[
            pltpu.VMEM((2, 4 * BLOCK, COLS), BF16),
            pltpu.VMEM((2 * BLOCK, COLS), BF16),
            pltpu.VMEM((2, 2, N_HI, 128, COLS), BF16),
            pltpu.VMEM((2, NY, N_HI, 32, COLS), BF16),
            pltpu.VMEM((2, NY, 64, COLS), BF16),
            pltpu.VMEM((2, NX, NY, 16, COLS), BF16),
            pltpu.VMEM((NZ, 16, COLS), BF16),
            pltpu.VMEM((2 * LOCAL_HEADS, BLOCK, HEAD_DIM), F32),
            pltpu.VMEM((2 * LOCAL_HEADS, BLOCK, 1), F32),
            pltpu.VMEM((2 * LOCAL_HEADS, BLOCK, 1), F32),
            pltpu.VMEM((2, BLOCK, COLS), BF16),
            dma((3,)), dma((3,)), dma((3,)),
            dma((2, LOCAL_HEADS, 2)), dma((2, LOCAL_HEADS, 2)),
            dma((1,)), dma((1,)), dma((NZ,)), dma((NZ,)), dma((3,)), dma((3,)),
            dma((4, 2)), dma((4, 2)), dma((4, 2)), dma((4, 2)),
            dma((NY, NX)), dma((NY, NX)),
            dma((LOCAL_HEADS,)), dma((LOCAL_HEADS,)), dma((LOCAL_HEADS,)),
        ],
        compiler_params=pltpu.CompilerParams(
            collective_id=0, has_side_effects=True, vmem_limit_bytes=48 * 1024 * 1024
        ),
    )(query_rows, key_rows, value_rows)


def solution(mesh):
    spec = P(("seqa", "seqb"), None)
    return jax.shard_map(
        local, mesh=mesh, in_specs=(spec, spec, spec), out_specs=spec, check_vma=False
    )
```

time: 347 us -> 157 us (0.45)
  the two profiles are of different devices: /device:TPU:49 before, /device:TPU:397 now
where the time goes in v1:
time: 157 us; the launch traced here: 156 us
  Pallas kernels  152 us (97%)
  local copies, waits for them, and re-layouts  3.92 us (2%)
    pallas_call x1, Pallas kernels, local(): pl.pallas_call(kernel, out_shape=jax.ShapeDtypeStruct(query_rows.shape, q...  152 us
    unnamed x7, local copies, waits for them, and re-layouts  3.92 us

profile of v1, /device:TPU:397, one launch (start us, length us, event | category | flops | bytes accessed | tf_op | source)
XLA Modules:
  0.0 156.4 jit_solution(8014309488669530332)
XLA Ops:
  0.0 0.0 copy-start
  0.0 1.0 copy-done
  1.0 0.0 copy-start.1
  1.0 1.0 copy-done.1
  2.1 0.0 copy-start.2
  2.1 1.0 copy-done.2
  3.1 152.5 %shard_map.37 = bf16[256,1024]{1,0:T(8,128)(2,1)S(1)} custom-call(bf16[256,1024]{1,0:T(8,128)(2,1)S(1)} %copy-done, bf16[256,1024]{1,0:T(8,128)(2,1)S(1)} %copy-done.1, bf16[256,1024]{1,0:T(8,128)(2,1)S(1)} %copy-done.2), custom_call_target="tpu_custom_call" | custom-call | tf_op jit(solution)/shard_map/pallas_call | solution.py:310
  155.6 0.8 copy.5
Async XLA Ops:
  0.0 1.0 copy-start
  1.0 1.0 copy-start.1
  2.1 1.0 copy-start.2

commit v2 on v1

v2 whole, which is shorter than its diff:
```python
import contextlib

import jax
import jax.numpy as jnp
from jax import lax
from jax.experimental import pallas as pl
from jax.experimental.pallas import tpu as pltpu
from jax.sharding import PartitionSpec as P

MESH = pl.DeviceIdType.MESH
BF16, F32 = jnp.bfloat16, jnp.float32

HEAD_DIM = 128
BLOCK = 256
NX, NY, NZ, NZ_LO, N_HI = 4, 8, 8, 4, 2
CHIPS = 256
LOCAL_HEADS = 4
COLS = LOCAL_HEADS * HEAD_DIM
EXP2_SCALE = 1.4426950408889634 / HEAD_DIM**0.5
MASKED = -1e30
EARLY = 0
WRAP_HEADS = (2, 3)


def scope(name):
    return contextlib.nullcontext()


def arrive(name, *copies):
    with scope(name):
        for copy in copies:
            copy.wait_recv()


def pool_matrix(rows, columns):
    row = lax.broadcasted_iota(jnp.int32, (rows, columns), 0)
    column = lax.broadcasted_iota(jnp.int32, (rows, columns), 1)
    return jnp.where((column >> 2) == row, 0.25, 0.0).astype(BF16)


def matmul(a, b):
    return jnp.dot(a, b, preferred_element_type=F32)


def kernel(
    q_hbm, k_hbm, v_hbm, o_hbm,
    near, queries, l1, l2, l3, l4, tile, acc, top, den, result,
    loc_sem, sib_s, sib_r, near_s, near_r, relay_s, relay_r, wrap_s, one_s, one_r, l2z_s, l2z_r, l3z_s, l3z_r, l1_s, l1_r,
    ring2_s, ring2_r, ring3_s, ring3_r, l4_s, l4_r, out_loc, out_s, out_r,
):
    seqa, seqb = lax.axis_index("seqa"), lax.axis_index("seqb")
    x, z_lo = seqa // NZ_LO, seqa % NZ_LO
    y, hi, core = seqb // 4, (seqb // 2) % 2, seqb % 2
    z = hi * NZ_LO + z_lo
    chip = seqa * 16 + seqb // 2

    def at_z(d):
        other = (z + d) % NZ
        return (x * NZ_LO + other % NZ_LO, (y * 2 + other // NZ_LO) * 2 + core)

    def at_y(d):
        return (seqa, (((y + d) % NY) * 2 + hi) * 2 + core)

    def at_x(d):
        return (((x + d) % NX) * NZ_LO + z_lo, seqb)

    sibling = (seqa, seqb + 1 - 2 * core)
    y_pair = (seqa, ((y + 1 - 2 * (y % 2)) * 2 + hi) * 2 + core)
    y_par = y % 2

    last = ((hi == 0) & (y == NY - 1)) | ((hi == 1) & (y == 0))
    first_of_row = ((hi == 0) & (y == 0)) | ((hi == 1) & (y == NY - 1))
    z_partner = at_z(4)
    rows_of_chips = NX * NZ_LO
    relay_to = (
        jnp.where(last, (seqa + rows_of_chips + 1 - 2 * hi) % rows_of_chips, seqa),
        at_y(NY + 1 - 2 * hi)[1],
    )
    relay_from = (
        jnp.where(first_of_row, (seqa + rows_of_chips + 2 * hi - 1) % rows_of_chips, seqa),
        at_y(NY + 2 * hi - 1)[1],
    )

    wraps = jnp.where(hi == 0, z_lo == NZ_LO - 1, z_lo == 0) & last
    owns_wrap = jnp.where(hi == 1, z_lo == NZ_LO - 1, z_lo == 0) & first_of_row
    takes_wrap = jnp.where(hi == 0, z_lo == 0, z_lo == NZ_LO - 1) & first_of_row
    wrap_to = (
        (seqa + rows_of_chips + 2 * hi - 1) % rows_of_chips,
        (((y + NY + 2 * hi - 1) % NY) * 2 + 1 - hi) * 2 + core,
    )
    wrap_from = wrap_to

    barrier = pltpu.get_barrier_semaphore()
    partners = [sibling, relay_from]
    partners += [at_z(d) for d in range(1, NZ)]
    partners += [at_y(d) for d in (1, 7)] + [at_x(d) for d in (1, 2, 3)]
    with scope("entry"):
        for partner in partners:
            pl.semaphore_signal(barrier, inc=1, device_id=partner, device_id_type=MESH)

        @pl.when(takes_wrap)
        def _():
            pl.semaphore_signal(barrier, inc=1, device_id=wrap_from, device_id_type=MESH)

        pl.semaphore_wait(barrier, len(partners) + jnp.where(owns_wrap, 1, 0))

    def remote(src, dst, s, r, device):
        return pltpu.make_async_remote_copy(
            src_ref=src, dst_ref=dst, send_sem=s, recv_sem=r, device_id=device, device_id_type=MESH
        )

    mine = pl.ds(pl.multiple_of(core * COLS, COLS), COLS)
    theirs = pl.ds(pl.multiple_of((1 - core) * COLS, COLS), COLS)
    own_rows = pl.ds(pl.multiple_of(core * BLOCK, BLOCK), BLOCK)
    sib_rows = pl.ds(pl.multiple_of((1 - core) * BLOCK, BLOCK), BLOCK)
    own_near = pl.ds(pl.multiple_of(BLOCK + core * BLOCK, BLOCK), BLOCK)
    sib_near = pl.ds(pl.multiple_of(2 * BLOCK - core * BLOCK, BLOCK), BLOCK)

    sib = [
        remote(k_hbm.at[:, theirs], near.at[0, own_near], sib_s.at[0], sib_r.at[0], sibling),
        remote(v_hbm.at[:, theirs], near.at[1, own_near], sib_s.at[1], sib_r.at[1], sibling),
        remote(q_hbm.at[:, theirs], queries.at[own_rows], sib_s.at[2], sib_r.at[2], sibling),
    ]
    loc = [
        pltpu.make_async_copy(k_hbm.at[:, mine], near.at[0, own_near], loc_sem.at[0]),
        pltpu.make_async_copy(v_hbm.at[:, mine], near.at[1, own_near], loc_sem.at[1]),
        pltpu.make_async_copy(q_hbm.at[:, mine], queries.at[own_rows], loc_sem.at[2]),
    ]
    for copy in (sib[0], sib[1], loc[0], loc[1], sib[2], loc[2]):
        copy.start()

    own_kind = 1 - (core + hi) % 2

    def near_copy(kind, head, t):
        columns = pl.ds(head * HEAD_DIM, HEAD_DIM)
        block = hi * kind + (1 - hi) * (1 - kind)
        src = near.at[t, pl.ds(pl.multiple_of(BLOCK + block * BLOCK, BLOCK), BLOCK), columns]
        place = 4 * BLOCK * kind + hi * 3 * BLOCK * (1 - kind)
        dst = near.at[t, pl.ds(pl.multiple_of(place, BLOCK), BLOCK), columns]
        return remote(src, dst, near_s.at[kind, head, t], near_r.at[kind, head, t], z_partner)

    loc[0].wait()
    near_first = near_copy(own_kind, 0, 0)
    near_first.start()
    loc[1].wait()
    arrive("sibling rows", sib[0], sib[1])

    tiles = []
    with scope("pooling"):
        for t in range(2):
            one = matmul(pool_matrix(128, 512), near[t, BLOCK : 3 * BLOCK, :]).astype(BF16)
            l1[t, y_par, hi] = one
            two = matmul(pool_matrix(32, 128), one).astype(BF16)
            l2[t, y, hi] = two
            tiles.append(matmul(pool_matrix(16, 32), two)[:8])
        tile[z] = jnp.concatenate(tiles, axis=0).astype(BF16)

    l3z = [
        remote(tile.at[z], tile.at[z], l3z_s.at[d], l3z_r.at[d], at_z(d)) for d in range(1, NZ)
    ]
    for copy in l3z:
        copy.start()
    l2z = remote(l2.at[:, y, hi], l2.at[:, y, hi], l2z_s.at[0], l2z_r.at[0], at_z(4))
    l2z.start()
    own_one = l1.at[:, y_par, hi]
    l1y = remote(own_one, own_one, l1_s.at[1], l1_r.at[1], y_pair)
    l1y.start()
    near_rest = [near_copy(1 - own_kind, 0, 0)] + [
        near_copy(kind, head, t)
        for kind in (1, 0)
        for head in range(LOCAL_HEADS)
        for t in range(2)
        if (head, t) != (0, 0)
    ]
    for copy in near_rest[:EARLY]:
        copy.start()

    def head_columns(head):
        return pl.ds(pl.multiple_of(head * HEAD_DIM, HEAD_DIM), HEAD_DIM)

    def attend(head, first_query, count, keys, values, allowed, first):
        q = queries[first_query : first_query + count, head_columns(head)]
        span = slice(first_query, first_query + count)
        scores = lax.dot_general(keys, q, (((1,), (1,)), ((), ())), preferred_element_type=F32)
        if allowed is not None:
            scores = jnp.where(allowed, scores, MASKED)
        highest = jnp.max(scores, axis=0, keepdims=True)
        if not first:
            old = top[head, :, span]
            highest = jnp.maximum(highest, old)
        weights = jnp.exp2((scores - highest) * EXP2_SCALE)
        total = jnp.sum(weights, axis=0, keepdims=True)
        mixed = lax.dot_general(
            values, weights.astype(BF16), (((0,), (0,)), ((), ())), preferred_element_type=F32
        )
        if not first:
            shrink = jnp.exp2((old - highest) * EXP2_SCALE)
            total = total + den[head, :, span] * shrink
            mixed = mixed + acc[head, :, span] * shrink
        top[head, :, span] = highest
        den[head, :, span] = total
        acc[head, :, span] = mixed

    loc[2].wait()
    sib[2].wait_recv()

    def inner(head, carry):
        columns = head_columns(head)
        key = lax.broadcasted_iota(jnp.int32, (2 * BLOCK, 2 * BLOCK), 0)
        query = lax.broadcasted_iota(jnp.int32, (2 * BLOCK, 2 * BLOCK), 1)
        allowed = (key <= query + BLOCK - 1) & (key >= query - BLOCK)
        keys, values = near[0, BLOCK : 3 * BLOCK, columns], near[1, BLOCK : 3 * BLOCK, columns]
        attend(head, 0, 2 * BLOCK, keys, values, allowed, True)
        return carry

    with scope("inner"):
        lax.fori_loop(0, LOCAL_HEADS, inner, 0, unroll=True)

    arrive("three along z", *l3z)
    arrive("two along z", l2z)
    wrap_copies = [
        remote(
            near.at[:, pl.ds(pl.multiple_of((1 + hi) * BLOCK, BLOCK), BLOCK), columns],
            near.at[:, pl.ds(pl.multiple_of((1 - hi) * 3 * BLOCK, BLOCK), BLOCK), columns],
            wrap_s.at[head], relay_r.at[head], wrap_to,
        )
        for head in WRAP_HEADS
        for columns in [pl.ds(head * HEAD_DIM, HEAD_DIM)]
    ]

    @pl.when(owns_wrap)
    def _():
        for copy in wrap_copies:
            copy.start()

    for copy in near_rest[EARLY:]:
        copy.start()
    for t in range(2):
        rows = [tile[i].astype(F32)[8 * t : 8 * t + 8] for i in range(NZ)]
        l3[t, y] = jnp.concatenate(rows, axis=0).astype(BF16)

    relays, one_parts = [], []

    def partner_one(kind, head):
        columns = pl.ds(head * HEAD_DIM, HEAD_DIM)
        block = (1 - hi) * kind + hi * (1 - kind)
        rows = pl.ds(pl.multiple_of(block * 64, 64), 64)
        place = 4 * BLOCK * kind + (1 - hi) * 3 * BLOCK * (1 - kind)

        for t in range(2):
            block_rows = near[t, pl.ds(pl.multiple_of(place, BLOCK), BLOCK), columns]
            pooled = matmul(pool_matrix(64, BLOCK), block_rows)
            l1[t, y_par, 1 - hi, rows, columns] = pooled.astype(BF16)
        part = l1.at[:, y_par, 1 - hi, rows, columns]
        copy = remote(part, part, one_s.at[kind, head], one_r.at[kind, head], y_pair)
        copy.start()
        one_parts.append(copy)

    def relay(head):
        columns = pl.ds(head * HEAD_DIM, HEAD_DIM)
        arrive("outer %d" % head, near_copy(1, head, 0), near_copy(1, head, 1))
        copy = remote(
            near.at[:, 4 * BLOCK :, columns],
            near.at[:, pl.ds(pl.multiple_of(hi * 3 * BLOCK, BLOCK), BLOCK), columns],
            relay_s.at[head], relay_r.at[head], relay_to,
        )
        relays.append(copy)
        if head in WRAP_HEADS:
            pl.when(jnp.logical_not(wraps))(lambda: copy.start())
        else:
            copy.start()
        partner_one(1, head)

    l4_copies = []

    def send_four(j, chunk):
        for t in range(2):
            l4[t, x, chunk] = matmul(pool_matrix(16, 64), l3[t, chunk]).astype(BF16)
        part = l4.at[:, x, chunk]
        for d in range(1, NX):
            copy = remote(part, part, l4_s.at[j, d], l4_r.at[j, d], at_x(d))
            copy.start()
            l4_copies.append(copy)

    def ring_step(buf, send, recv, s):
        up, down = (y - (s - 1) + NY) % NY, (y + s - 1) % NY
        if s < 4:
            up, down = buf.at[:, up], buf.at[:, down]
        else:
            up, down = buf.at[0, up], buf.at[1, down]
        copies = [
            remote(up, up, send.at[s - 1, 0], recv.at[s - 1, 0], at_y(1)),
            remote(down, down, send.at[s - 1, 1], recv.at[s - 1, 1], at_y(NY - 1)),
        ]
        for copy in copies:
            copy.start()
        return copies

    ring3 = ring_step(l3, ring3_s, ring3_r, 1)
    send_four(0, y)
    ring2 = ring_step(l2, ring2_s, ring2_r, 1)
    finished = list(ring3) + list(ring2)
    for s in range(1, 5):
        arrive("ring3 %d" % s, *ring3)
        if s < 4:
            ring3 = ring_step(l3, ring3_s, ring3_r, s + 1)
            finished += ring3
            send_four(2 * s - 1, (y - s + NY) % NY)
            send_four(2 * s, (y + s) % NY)
        else:
            send_four(7, (y + 4) % NY)
        arrive("ring2 %d" % s, *ring2)
        if s < 4:
            ring2 = ring_step(l2, ring2_s, ring2_r, s + 1)
            finished += ring2
    def far_keys(buf, columns):
        index = (slice(None),) * (len(buf.shape) - 2) + (columns,)
        return [buf[(t,) + index].reshape(512, HEAD_DIM) for t in range(2)]

    def far(buf):
        def body(head, carry):
            attend(head, 0, 2 * BLOCK, *far_keys(buf, head_columns(head)), None, False)
            return carry

        with scope("far"):
            lax.fori_loop(0, LOCAL_HEADS, body, 0, unroll=True)

    for head in range(LOCAL_HEADS):
        relay(head)
    far(l3)
    far(l2)
    arrive("four along x", *l4_copies)
    far(l4)
    arrive("one along y", l1y)

    out = []

    def finish(head):
        columns = pl.ds(head * HEAD_DIM, HEAD_DIM)
        arrive("relay %d" % head, relays[head])
        key = lax.broadcasted_iota(jnp.int32, (BLOCK, BLOCK), 0)
        query = lax.broadcasted_iota(jnp.int32, (BLOCK, BLOCK), 1)
        for half in range(2):
            edge = slice(half * 3 * BLOCK, half * 3 * BLOCK + BLOCK)
            if half == 0:
                allowed = (key >= query) & (chip > 0)
            else:
                allowed = (key < query) & (chip < CHIPS - 1)
            attend(
                head, half * BLOCK, BLOCK, near[0, edge, columns], near[1, edge, columns],
                allowed, False,
            )
        arrive("one %d" % head, one_parts[head], one_parts[LOCAL_HEADS + head])
        attend(head, 0, 2 * BLOCK, *far_keys(l1, columns), None, False)
        mean = (acc[head] / den[head]).T.astype(BF16)
        for half in range(2):
            result[half, :, columns] = mean[half * BLOCK : (half + 1) * BLOCK]
        place = pl.ds(pl.multiple_of(core * COLS + head * HEAD_DIM, HEAD_DIM), HEAD_DIM)
        away = remote(
            result.at[1 - core, :, columns], o_hbm.at[:, place],
            out_s.at[head], out_r.at[head], sibling,
        )
        away.start()
        here = pltpu.make_async_copy(
            result.at[core, :, columns], o_hbm.at[:, place], out_loc.at[head]
        )
        here.start()
        out.append((away, here))

    for head in range(LOCAL_HEADS + 1):
        if head < LOCAL_HEADS:
            arrive("inner %d" % head, near_copy(0, head, 0), near_copy(0, head, 1))
            partner_one(0, head)
        if head > 0:
            finish(head - 1)
    with scope("sent"):
        for copy in sib + l3z + [l2z, l1y, near_first] + near_rest + finished + l4_copies:
            copy.wait_send()
        for copy in one_parts:
            copy.wait_send()
        for head in range(LOCAL_HEADS):
            if head not in WRAP_HEADS:
                relays[head].wait_send()

        @pl.when(jnp.logical_not(wraps))
        def _():
            for head in WRAP_HEADS:
                relays[head].wait_send()

        @pl.when(owns_wrap)
        def _():
            for copy in wrap_copies:
                copy.wait_send()

    with scope("result"):
        for away, here in out:
            here.wait()
            away.wait()


def local(query_rows, key_rows, value_rows):
    any_space = pl.BlockSpec(memory_space=pl.ANY)
    dma = pltpu.SemaphoreType.DMA
    return pl.pallas_call(
        kernel,
        out_shape=jax.ShapeDtypeStruct(query_rows.shape, query_rows.dtype),
        in_specs=[pl.BlockSpec(memory_space=pltpu.HBM)] * 3,
        out_specs=any_space,
        scratch_shapes=[
            pltpu.VMEM((2, 5 * BLOCK, COLS), BF16),
            pltpu.VMEM((2 * BLOCK, COLS), BF16),
            pltpu.VMEM((2, 2, N_HI, 128, COLS), BF16),
            pltpu.VMEM((2, NY, N_HI, 32, COLS), BF16),
            pltpu.VMEM((2, NY, 64, COLS), BF16),
            pltpu.VMEM((2, NX, NY, 16, COLS), BF16),
            pltpu.VMEM((NZ, 16, COLS), BF16),
            pltpu.VMEM((LOCAL_HEADS, HEAD_DIM, 2 * BLOCK), F32),
            pltpu.VMEM((LOCAL_HEADS, 1, 2 * BLOCK), F32),
            pltpu.VMEM((LOCAL_HEADS, 1, 2 * BLOCK), F32),
            pltpu.VMEM((2, BLOCK, COLS), BF16),
            dma((3,)), dma((3,)), dma((3,)),
            dma((2, LOCAL_HEADS, 2)), dma((2, LOCAL_HEADS, 2)),
            dma((LOCAL_HEADS,)), dma((LOCAL_HEADS,)), dma((LOCAL_HEADS,)), dma((2, LOCAL_HEADS)), dma((2, LOCAL_HEADS)),
            dma((1,)), dma((1,)), dma((NZ,)), dma((NZ,)), dma((3,)), dma((3,)),
            dma((4, 2)), dma((4, 2)), dma((4, 2)), dma((4, 2)),
            dma((NY, NX)), dma((NY, NX)),
            dma((LOCAL_HEADS,)), dma((LOCAL_HEADS,)), dma((LOCAL_HEADS,)),
        ],
        compiler_params=pltpu.CompilerParams(
            collective_id=0, has_side_effects=True, vmem_limit_bytes=53 * 1024 * 1024
        ),
    )(query_rows, key_rows, value_rows)


def solution(mesh):
    spec = P(("seqa", "seqb"), None)
    return jax.shard_map(
        local, mesh=mesh, in_specs=(spec, spec, spec), out_specs=spec, check_vma=False
    )
```

time: 157 us -> 91.3 us (0.58)
  the two profiles are of different devices: /device:TPU:397 before, /device:TPU:141 now
where the time goes in v2:
time: 91.3 us; the launch traced here: 91.2 us
  Pallas kernels  90.4 us (99%)
    pallas_call x1, Pallas kernels, local(): pl.pallas_call(kernel, out_shape=jax.ShapeDtypeStruct(query_rows.shape, q...  90.4 us

profile of v2, /device:TPU:141, one launch (start us, length us, event | category | flops | bytes accessed | tf_op | source)
XLA Modules:
  0.0 91.2 jit_solution(17856068975223303579)
XLA Ops:
  0.0 90.4 %shard_map.37 = bf16[256,1024]{1,0:T(8,128)(2,1)S(1)} custom-call(bf16[256,1024]{1,0:T(8,128)(2,1)} %q_hbm.1, bf16[256,1024]{1,0:T(8,128)(2,1)} %k_hbm.1, bf16[256,1024]{1,0:T(8,128)(2,1)} %v_hbm.1), custom_call_target="tpu_custom_call" | custom-call | tf_op jit(solution)/shard_map/pallas_call | solution.py:404
  90.4 0.8 copy.5

commit v3 on v2

--- a/solution.py
+++ b/solution.py
@@ -18,8 +18,8 @@
 COLS = LOCAL_HEADS * HEAD_DIM
 EXP2_SCALE = 1.4426950408889634 / HEAD_DIM**0.5
 MASKED = -1e30
-EARLY = 0
-WRAP_HEADS = (2, 3)
+EARLY, LATE = 0, 8
+WRAP_HEADS = (3,)
 
 
 def scope(name):
@@ -45,7 +45,7 @@
 def kernel(
     q_hbm, k_hbm, v_hbm, o_hbm,
     near, queries, l1, l2, l3, l4, tile, acc, top, den, result,
-    loc_sem, sib_s, sib_r, near_s, near_r, relay_s, relay_r, wrap_s, one_s, one_r, l2z_s, l2z_r, l3z_s, l3z_r, l1_s, l1_r,
+    loc_sem, sib_s, sib_r, near_s, near_r, relay_s, relay_r, wrap_s, shift_s, shift_r, onward_s, one_s, one_r, l2z_s, l2z_r, l3z_s, l3z_r, l1_s, l1_r,
     ring2_s, ring2_r, ring3_s, ring3_r, l4_s, l4_r, out_loc, out_s, out_r,
 ):
     seqa, seqb = lax.axis_index("seqa"), lax.axis_index("seqb")
@@ -84,6 +84,7 @@
     wraps = jnp.where(hi == 0, z_lo == NZ_LO - 1, z_lo == 0) & last
     owns_wrap = jnp.where(hi == 1, z_lo == NZ_LO - 1, z_lo == 0) & first_of_row
     takes_wrap = jnp.where(hi == 0, z_lo == 0, z_lo == NZ_LO - 1) & first_of_row
+    shifted = jnp.where(hi == 0, z_lo > 0, z_lo < NZ_LO - 1) & last
     wrap_to = (
         (seqa + rows_of_chips + 2 * hi - 1) % rows_of_chips,
         (((y + NY + 2 * hi - 1) % NY) * 2 + 1 - hi) * 2 + core,
@@ -233,7 +234,7 @@
         for copy in wrap_copies:
             copy.start()
 
-    for copy in near_rest[EARLY:]:
+    for copy in near_rest[EARLY:LATE]:
         copy.start()
     for t in range(2):
         rows = [tile[i].astype(F32)[8 * t : 8 * t + 8] for i in range(NZ)]
@@ -256,17 +257,33 @@
         copy.start()
         one_parts.append(copy)
 
+    def shift_copy(head):
+        columns = pl.ds(head * HEAD_DIM, HEAD_DIM)
+        return remote(
+            near.at[:, 4 * BLOCK : 5 * BLOCK, columns], near.at[:, 5 * BLOCK :, columns],
+            shift_s.at[head], shift_r.at[head], at_z(NZ + 1 - 2 * hi),
+        )
+
+    def onward_copy(head):
+        columns = pl.ds(head * HEAD_DIM, HEAD_DIM)
+        return remote(
+            near.at[:, 5 * BLOCK :, columns],
+            near.at[:, pl.ds(pl.multiple_of(hi * 3 * BLOCK, BLOCK), BLOCK), columns],
+            onward_s.at[head], relay_r.at[head], at_y(NY + 1 - 2 * hi),
+        )
+
     def relay(head):
         columns = pl.ds(head * HEAD_DIM, HEAD_DIM)
         arrive("outer %d" % head, near_copy(1, head, 0), near_copy(1, head, 1))
         copy = remote(
-            near.at[:, 4 * BLOCK :, columns],
+            near.at[:, 4 * BLOCK : 5 * BLOCK, columns],
             near.at[:, pl.ds(pl.multiple_of(hi * 3 * BLOCK, BLOCK), BLOCK), columns],
             relay_s.at[head], relay_r.at[head], relay_to,
         )
         relays.append(copy)
         if head in WRAP_HEADS:
-            pl.when(jnp.logical_not(wraps))(lambda: copy.start())
+            pl.when(jnp.logical_not(last))(lambda: copy.start())
+            pl.when(last & jnp.logical_not(wraps))(lambda: shift_copy(head).start())
         else:
             copy.start()
         partner_one(1, head)
@@ -327,8 +344,17 @@
 
     for head in range(LOCAL_HEADS):
         relay(head)
+    for copy in near_rest[LATE:]:
+        copy.start()
+
     far(l3)
     far(l2)
+    @pl.when(shifted)
+    def _():
+        for head in WRAP_HEADS:
+            shift_copy(head).wait_recv()
+            onward_copy(head).start()
+
     arrive("four along x", *l4_copies)
     far(l4)
     arrive("one along y", l1y)
@@ -382,10 +408,20 @@
             if head not in WRAP_HEADS:
                 relays[head].wait_send()
 
-        @pl.when(jnp.logical_not(wraps))
+        @pl.when(jnp.logical_not(last))
         def _():
             for head in WRAP_HEADS:
                 relays[head].wait_send()
+
+        @pl.when(last & jnp.logical_not(wraps))
+        def _():
+            for head in WRAP_HEADS:
+                shift_copy(head).wait_send()
+
+        @pl.when(shifted)
+        def _():
+            for head in WRAP_HEADS:
+                onward_copy(head).wait_send()
 
         @pl.when(owns_wrap)
         def _():
@@ -407,7 +443,7 @@
         in_specs=[pl.BlockSpec(memory_space=pltpu.HBM)] * 3,
         out_specs=any_space,
         scratch_shapes=[
-            pltpu.VMEM((2, 5 * BLOCK, COLS), BF16),
+            pltpu.VMEM((2, 6 * BLOCK, COLS), BF16),
             pltpu.VMEM((2 * BLOCK, COLS), BF16),
             pltpu.VMEM((2, 2, N_HI, 128, COLS), BF16),
             pltpu.VMEM((2, NY, N_HI, 32, COLS), BF16),
@@ -420,6 +456,7 @@
             pltpu.VMEM((2, BLOCK, COLS), BF16),
             dma((3,)), dma((3,)), dma((3,)),
             dma((2, LOCAL_HEADS, 2)), dma((2, LOCAL_HEADS, 2)),
+            dma((LOCAL_HEADS,)), dma((LOCAL_HEADS,)), dma((LOCAL_HEADS,)),
             dma((LOCAL_HEADS,)), dma((LOCAL_HEADS,)), dma((LOCAL_HEADS,)), dma((2, LOCAL_HEADS)), dma((2, LOCAL_HEADS)),
             dma((1,)), dma((1,)), dma((NZ,)), dma((NZ,)), dma((3,)), dma((3,)),
             dma((4, 2)), dma((4, 2)), dma((4, 2)), dma((4, 2)),

time: 91.3 us -> 86.4 us (0.946)
  the two profiles are of different devices: /device:TPU:141 before, /device:TPU:247 now
where the time goes in v3:
time: 86.4 us; the launch traced here: 86.2 us
  Pallas kernels  85.4 us (99%)
    pallas_call x1, Pallas kernels, local(): pl.pallas_call(kernel, out_shape=jax.ShapeDtypeStruct(query_rows.shape, q...  85.4 us

profile of v3, /device:TPU:247, one launch (start us, length us, event | category | flops | bytes accessed | tf_op | source)
XLA Modules:
  0.0 86.2 jit_solution(8149703902758388239)
XLA Ops:
  0.0 85.4 %shard_map.37 = bf16[256,1024]{1,0:T(8,128)(2,1)S(1)} custom-call(bf16[256,1024]{1,0:T(8,128)(2,1)} %q_hbm.1, bf16[256,1024]{1,0:T(8,128)(2,1)} %k_hbm.1, bf16[256,1024]{1,0:T(8,128)(2,1)} %v_hbm.1), custom_call_target="tpu_custom_call" | custom-call | tf_op jit(solution)/shard_map/pallas_call | solution.py:440
  85.4 0.8 copy.5

commit v4 on v3

--- a/solution.py
+++ b/solution.py
@@ -343,8 +343,10 @@
             lax.fori_loop(0, LOCAL_HEADS, body, 0, unroll=True)
 
     for head in range(LOCAL_HEADS):
+        if head == LOCAL_HEADS - 1:
+            near_rest[LATE].start()
         relay(head)
-    for copy in near_rest[LATE:]:
+    for copy in near_rest[LATE + 1 :]:
         copy.start()
 
     far(l3)

time: 86.4 us -> 86.4 us (level)
  no operation moved by 1% of the time
where the time goes in v4:
time: 86.4 us; the launch traced here: 86.3 us
  Pallas kernels  85.5 us (99%)
    pallas_call x1, Pallas kernels, local(): pl.pallas_call(kernel, out_shape=jax.ShapeDtypeStruct(query_rows.shape, q...  85.5 us

profile of v4, /device:TPU:247, one launch (start us, length us, event | category | flops | bytes accessed | tf_op | source)
XLA Modules:
  0.0 86.3 jit_solution(1237624440709876926)
XLA Ops:
  0.0 85.5 %shard_map.37 = bf16[256,1024]{1,0:T(8,128)(2,1)S(1)} custom-call(bf16[256,1024]{1,0:T(8,128)(2,1)} %q_hbm.1, bf16[256,1024]{1,0:T(8,128)(2,1)} %k_hbm.1, bf16[256,1024]{1,0:T(8,128)(2,1)} %v_hbm.1), custom_call_target="tpu_custom_call" | custom-call | tf_op jit(solution)/shard_map/pallas_call | solution.py:442
  85.5 0.8 copy.5
